TPU v7x, 256 devices: a whole 4x4x8 slice. The times are simulated.
256 devices in a mesh: dp: 16 (over z, x_hi), tensor: 16 (over x_lo, y, core).
Axes of the slice: x: 4 (x_hi: 2, x_lo: 2; x = x_hi * 2 + x_lo), y: 4, z: 8, core: 2. Of those that a mesh axis runs over, the one named last changes fastest.
Arguments:
- tokens: bfloat16 [256, 16384], P('dp'), may hold values from -6 to 6
- gate_codes: bfloat16 [16384, 26624], P('dp', 'tensor'), may hold values from 0 to 255, as said below
- gate_scales: bfloat16 [128, 53248], P('dp', 'tensor'), may hold values from 0.00077819824 to 0.003112793
- up_codes: bfloat16 [16384, 26624], P('dp', 'tensor'), may hold values from 0 to 255, as said below
- up_scales: bfloat16 [128, 53248], P('dp', 'tensor'), may hold values from 0.00077819824 to 0.003112793
- down_codes: bfloat16 [53248, 8192], P('tensor', 'dp'), may hold values from 0 to 255, as said below
- down_scales: bfloat16 [416, 16384], P('tensor', 'dp'), may hold values from 0.00043296814 to 0.0017318726
- sign_bits: int32 [3328, 208], P('dp'), may hold values from 0 to 65535
Outputs:
- mixed: bfloat16 [256, 16384], P('tensor', 'dp')
- token_absmax: float32 [256], P('dp')
Inputs may be any that keep to these rules, and one draw needn't show every extreme that they name: `gate_codes`: whole numbers; entry w of a row holds the codes of columns 2 w (low four bits) and 2 w + 1 (high four bits); every bit is random. `up_codes`: same layout as gate_codes. `down_codes`: same layout as gate_codes, over the columns of the model width. `sign_bits`: bit k of word w in row a is the sign bit of column 16 w + k; every bit is random.
All inputs are finite; a program needn't handle non-finite values.
Results may differ from a plain program's by a relative error of at most 0.039.
Values may be sent and summed in bfloat16 or wider, within the bound.
A program may use at most 128 MiB of HBM per device.

v0:
```python
import math

import jax
import jax.numpy as jnp
from jax import lax
from jax.sharding import PartitionSpec as P

FF = 53248
GROUP = 128


def from_partner(value, axis, bit):
    mask = 2**bit
    pairs = [(source, source ^ mask) for source in range(lax.axis_size(axis))]
    return lax.ppermute(value, axis, pairs)


def dequant(packed, scales, group_size):
    row_count, word_count = packed.shape
    scale_grid = scales.astype(jnp.float32).reshape(row_count // group_size, 1, word_count, 2)
    whole = packed.astype(jnp.int32).reshape(row_count // group_size, group_size, word_count, 1)
    shifts = jnp.array([0, 4], jnp.int32).reshape(1, 1, 1, 2)
    code_vals = jnp.bitwise_and(jnp.right_shift(whole, shifts), 15) - 8
    values = (code_vals.astype(jnp.float32) * scale_grid).astype(jnp.bfloat16)
    return values.reshape(row_count, word_count * 2)


def unpack_signs(sign_bits):
    row_count, word_count = sign_bits.shape
    shifts = jnp.arange(16, dtype=jnp.int32).reshape(1, 1, 16)
    flag = jnp.bitwise_and(jnp.right_shift(sign_bits[:, :, None], shifts), 1)
    return (1 - 2 * flag).astype(jnp.bfloat16).reshape(row_count, word_count * 16)


def local(tokens, gate_codes, gate_scales, up_codes, up_scales, down_codes, down_scales, sign_bits):
    block_hidden = gate_scales.shape[1]
    all_sign_bits = lax.all_gather(sign_bits, "dp", axis=0, tiled=True)
    feature_rows = lax.all_to_all(tokens, "dp", split_axis=1, concat_axis=0, tiled=True)
    gate_dense = dequant(gate_codes, gate_scales, GROUP)
    up_dense = dequant(up_codes, up_scales, GROUP)
    left = feature_rows
    both_sums = lax.psum_scatter(
        jnp.concatenate(
            [
                jnp.dot(left, gate_dense, preferred_element_type=jnp.float32),
                jnp.dot(left, up_dense, preferred_element_type=jnp.float32),
            ],
            axis=1,
        ).astype(jnp.bfloat16),
        "dp",
        scatter_dimension=0,
        tiled=True,
    ).astype(jnp.float32)
    gate_sum = both_sums[:, :block_hidden]
    up_sum = both_sums[:, block_hidden:]
    hidden = (jax.nn.silu(gate_sum) * up_sum).astype(jnp.bfloat16)
    signs = unpack_signs(all_sign_bits)
    turned = lax.dot_general(
        hidden, signs, (((1,), (1,)), ((), ())), preferred_element_type=jnp.float32
    )
    group_count = lax.axis_size("tensor")
    position = lax.axis_index("tensor")
    for bit_pos in range(group_count.bit_length() - 1):
        partner = from_partner(turned.astype(jnp.bfloat16), "tensor", bit_pos).astype(turned.dtype)
        high_bit = jnp.bitwise_and(jnp.right_shift(position, bit_pos), 1)
        turned = jnp.where(high_bit == 1, partner - turned, turned + partner)
    rotated = (turned * (1.0 / math.sqrt(FF))).astype(jnp.bfloat16)
    local_peak = jnp.max(jnp.abs(rotated.astype(jnp.float32)), axis=1)
    token_absmax = lax.pmax(local_peak, "tensor")
    all_rotated = lax.all_gather(rotated, "dp", axis=0, tiled=True)
    down_dense = dequant(down_codes, down_scales, GROUP)
    left = all_rotated
    output = lax.psum_scatter(
        jnp.dot(left, down_dense, preferred_element_type=jnp.float32).astype(jnp.bfloat16),
        "tensor",
        scatter_dimension=0,
        tiled=True,
    )
    return (output, token_absmax)


def solution(mesh):
    return jax.shard_map(
        local,
        mesh=mesh,
        in_specs=(
            P("dp", None),
            P("dp", "tensor"),
            P("dp", "tensor"),
            P("dp", "tensor"),
            P("dp", "tensor"),
            P("tensor", "dp"),
            P("tensor", "dp"),
            P("dp", None),
        ),
        out_specs=(P("tensor", "dp"), P("dp")),
        check_vma=False,
    )
```

profile of v0, /device:TPU:1, one launch (start us, length us, event | category | flops | bytes accessed | tf_op | source)
XLA Modules:
  0.0 560.4 jit_solution(1830070349606741146)
XLA Ops:
  9.1 11.6 %all-to-all-start = ((bf16[16,16,1024]{2,0,1:T(8,128)(2,1)}), bf16[16,16,1024]{2,0,1:T(8,128)(2,1)}, u32[]{:S(2)}, u32[]{:S(2)}) async-start(bf16[16,16,1024]{2,0,1:T(8,128)(2,1)} %bitcast.84), calls=%async_computation | async-start | bytes 1048576 | tf_op jit(solution)/shard_map/all_to_all | solution.py:38
  21.5 5.5 convert.16
  27.0 7.8 %copy.36 = s32[8,128,1664]{1,0,2:T(8,128)} copy(s32[8,128,1664]{2,1,0:T(8,128)} %convert.16) | data formatting | bytes 13631488 | tf_op jit(solution)/shard_map/shift_right_arithmetic | solution.py:23
  34.8 3.4 convert.17
  38.2 7.7 %copy.39 = s32[8,128,1664]{1,0,2:T(8,128)} copy(s32[8,128,1664]{2,1,0:T(8,128)} %convert.17) | data formatting | bytes 13631488 | tf_op jit(solution)/shard_map/shift_right_arithmetic | solution.py:23
  46.6 11.0 %multiply_convert_fusion.1 = (bf16[8,128,1664,2]{1,0,3,2:T(8,128)(2,1)}, bf16[8,128,1664,2]{1,0,3,2:T(8,128)(2,1)}) fusion(f32[8,1664,2]{0,2,1:T(2,128)S(1)} %bitcast.89, s32[2]{0:T(128)S(1)} %iota_multiply_fusion, s32[8,128,1664]{1,0,2:T(8,128)} %copy.36, f32[8,1664,2]{0,2,1:T(2,128)S(1)} %bitcast.90, s32[8,128,1664]{1,0,2:T(8,128)} %copy.39), kind=kLoop, calls=%fused_computation.12 | loop fusion | flops 40894464 | bytes 27475976 | tf_op jit(solution)/shard_map/convert_element_type | solution.py:24
  57.5 5.1 fusion.22
  62.7 3.0 fusion.25
  65.9 4.4 copy.45
  70.5 46.8 %all-gather.3.cloned.1.call-done = s32[3328,208]{1,0:T(8,128)} async-done(((s32[208,208]{1,0:T(8,128)}), s32[3328,208]{1,0:T(8,128)}) %all-gather.3.cloned.1.call-update) | async-done | bytes 2768912 | tf_op jit(solution)/shard_map/all_gather | solution.py:37
  119.8 10.9 %fusion.3 = bf16[3328,3328]{0,1:T(8,128)(2,1)} fusion(s32[3328]{0:T(1024)S(1)} %shift_right_arithmetic.126, s32[3328,208]{0,1:T(8,128)S(1)} %copy.42), kind=kLoop, calls=%fused_computation.4 | loop fusion | flops 55377920 | bytes 24933376 | tf_op jit(solution)/shard_map/convert_element_type | solution.py:32
  130.7 197.8 %reduce-scatter.7.cloned.1.call-done = bf16[16,6656]{1,0:T(8,128)(2,1)} async-done(((bf16[256,6656]{1,0:T(8,128)(2,1)}), bf16[16,6656]{1,0:T(8,128)(2,1)}) %reduce-scatter.7.cloned.1.call-update) | async-done | bytes 213008 | tf_op jit(solution)/shard_map/reduce_scatter | solution.py:42
  329.5 9.8 %fusion.49 = (bf16[16,3328]{1,0:T(8,128)(2,1)}, f32[16,3328]{1,0:T(8,128)}) fusion(bf16[3328,3328]{0,1:T(8,128)(2,1)} %fusion.3, f32[16,6656]{1,0:T(8,128)S(1)} %convert_element_type.112), kind=kOutput, calls=%fused_computation.53 | convolution fusion | flops 354791424 | bytes 22896640 | tf_op jit(solution)/shard_map/dot_general | solution.py:58
  339.3 4.5 collective-permute-start
  347.8 3.3 collective-permute-done.1
  360.1 3.6 collective-permute-done.3
  367.4 3.9 convert.18
  371.3 10.3 %copy.43 = s32[26,128,512]{1,0,2:T(8,128)} copy(s32[26,128,512]{2,1,0:T(8,128)} %convert.18) | data formatting | bytes 13631488 | tf_op jit(solution)/shard_map/shift_right_arithmetic | solution.py:23
  381.7 64.2 %all-gather.5.cloned.1.call-done = bf16[256,3328]{1,0:T(8,128)(2,1)} async-done(((bf16[16,3328]{1,0:T(8,128)(2,1)}), bf16[256,3328]{1,0:T(8,128)(2,1)}) %all-gather.5.cloned.1.call-update) | async-done | bytes 1703952 | tf_op jit(solution)/shard_map/all_gather | solution.py:70
  445.9 11.8 %shift_right_arithmetic.131 = s32[26,128,512,2]{1,0,3,2:T(8,128)} broadcast(s32[26,128,512]{1,0,2:T(8,128)} %copy.43), dimensions={0,1,2} | broadcast | bytes 20447232 | tf_op jit(solution)/shard_map/shift_right_arithmetic | solution.py:23
  457.7 6.6 %mul.94 = f32[26,128,512,2]{1,0,3,2:T(8,128)} broadcast(f32[26,512,2]{0,2,1:T(2,128)S(1)} %bitcast.94), dimensions={0,2,3} | broadcast | bytes 13737984 | tf_op jit(solution)/shard_map/mul | solution.py:24
  464.3 29.2 %fusion.28 = bf16[256,1024]{1,0:T(8,128)(2,1)} fusion(bf16[256,3328]{1,0:T(8,128)(2,1)S(1)} %copy-done.3, f32[128,8,26,128]{3,2,1,0:T(8,128)} %bitcast.86, s32[128,8,26,128]{3,2,1,0:T(8,128)} %bitcast.85, s32[1024]{0:T(1024)S(1)} %shift_right_arithmetic.134), kind=kOutput, calls=%fused_computation.25 | convolution fusion | flops 1765539840 | bytes 29495296 | tf_op jit(solution)/shard_map/dot_general | solution.py:74
  493.5 31.3 %pmax.7 = f32[16]{0:T(128)} all-reduce(f32[16]{0:T(128)S(1)} %get-tuple-element.2), channel_id=1, replica_groups=mesh['dp'=16,'tensor'=16] {'tensor'}, use_global_device_ids=true, to_apply=%region_3.4 | all-reduce | flops 16 | bytes 128 | tf_op jit(solution)/shard_map/pmax | solution.py:69
  524.8 29.1 %reduce-scatter.5.cloned.1.call-done = bf16[16,1024]{1,0:T(8,128)(2,1)} async-done(((bf16[256,1024]{1,0:T(8,128)(2,1)}), bf16[16,1024]{1,0:T(8,128)(2,1)}) %reduce-scatter.5.cloned.1.call-update) | async-done | bytes 32784 | tf_op jit(solution)/shard_map/reduce_scatter | solution.py:73
  (44 shorter events, 23.9 us)
Async XLA Ops:
  9.1 48.4 %all-to-all-start = ((bf16[16,16,1024]{2,0,1:T(8,128)(2,1)}), bf16[16,16,1024]{2,0,1:T(8,128)(2,1)}, u32[]{:S(2)}, u32[]{:S(2)}) async-start(bf16[16,16,1024]{2,0,1:T(8,128)(2,1)} %bitcast.84), calls=%async_computation | async-start | bytes 1048576 | tf_op jit(solution)/shard_map/all_to_all | solution.py:38
  20.7 96.6 %all-gather.3.cloned.1.call-start = ((), (), s32[]{:S(2)}) async-start(), calls=%async_computation.3 | async-start | bytes 3620864 | tf_op jit(solution)/shard_map/all_gather | solution.py:37
  21.4 307.1 %reduce-scatter.7.cloned.1.call-start = ((), (), s32[]{:S(2)}) async-start(), calls=%async_computation.6 | async-start | bytes 3620864 | tf_op jit(solution)/shard_map/reduce_scatter | solution.py:42
  27.0 7.8 %copy-start.1 = (bf16[1024,1664]{1,0:T(8,128)(2,1)S(1)}, bf16[1024,1664]{1,0:T(8,128)(2,1)}, u32[]{:S(2)}) copy-start(bf16[1024,1664]{1,0:T(8,128)(2,1)} %param.14) | copy-start | bytes 10223620
  38.2 7.7 %copy-start.5 = (bf16[8,3328]{1,0:T(8,128)(2,1)S(1)}, bf16[8,3328]{1,0:T(8,128)(2,1)}, u32[]{:S(2)}) copy-start(bf16[8,3328]{1,0:T(8,128)(2,1)} %param.13) | copy-start | bytes 159748
  38.2 8.0 %copy-start.6 = (bf16[8,3328]{1,0:T(8,128)(2,1)S(1)}, bf16[8,3328]{1,0:T(8,128)(2,1)}, u32[]{:S(2)}) copy-start(bf16[8,3328]{1,0:T(8,128)(2,1)} %param.15) | copy-start | bytes 159748
  57.5 5.2 copy-start
  70.4 375.6 %all-gather.5.cloned.1.call-start = ((), (), s32[]{:S(2)}) async-start(), calls=%async_computation.4 | async-start | bytes 1810432 | tf_op jit(solution)/shard_map/all_gather | solution.py:70
  329.5 37.8 %copy-start.2 = (bf16[3328,512]{1,0:T(8,128)(2,1)S(1)}, bf16[3328,512]{1,0:T(8,128)(2,1)}, u32[]{:S(2)}) copy-start(bf16[3328,512]{1,0:T(8,128)(2,1)} %param.16) | copy-start | bytes 10223620
  339.3 5.7 %collective-permute-start = (bf16[16,3328]{1,0:T(8,128)(2,1)}, bf16[16,3328]{1,0:T(8,128)(2,1)S(1)}, u32[]{:S(2)}, u32[]{:S(2)}) collective-permute-start(bf16[16,3328]{1,0:T(8,128)(2,1)} %get-tuple-element.8), channel_id=1, source_target_pairs={{0,1},{1,0},{2,3},{3,2},{4,5},{5,4},{6,7},{7,6},{8,9},{9,8},{10,11... | collective-permute-start | bytes 319496 | tf_op jit(solution)/shard_map/ppermute | solution.py:15
  346.6 4.5 collective-permute-start.1
  352.9 5.3 collective-permute-start.2
  359.8 3.9 collective-permute-start.3
  365.5 188.4 %reduce-scatter.5.cloned.1.call-start = ((), (), s32[]{:S(2)}) async-start(), calls=%async_computation.5 | async-start | bytes 557056 | tf_op jit(solution)/shard_map/reduce_scatter | solution.py:73
  371.3 10.3 %copy-start.4 = (bf16[26,1024]{1,0:T(8,128)(2,1)S(1)}, bf16[26,1024]{1,0:T(8,128)(2,1)}, u32[]{:S(2)}) copy-start(bf16[26,1024]{1,0:T(8,128)(2,1)} %param.17) | copy-start | bytes 159748
  457.7 6.6 %copy-start.3 = (bf16[256,3328]{1,0:T(8,128)(2,1)S(1)}, bf16[256,3328]{1,0:T(8,128)(2,1)}, u32[]{:S(2)}) copy-start(bf16[256,3328]{1,0:T(8,128)(2,1)} %all-gather.5.cloned.1.call-done) | copy-start | bytes 5111812
Sparse Core Ops, SparseCore 0:
  24.1 93.1 all-gather.2
  121.3 207.1 reduce-scatter.6
  365.6 80.2 all-gather.4
  493.6 60.1 reduce-scatter.4
where the time goes:
time: 563 us; the launch traced here: 560 us
  waiting for transfers between devices  349 us (62%)
  local copies, waits for them, and re-layouts  55.7 us (10%)
  matrix products  47.1 us (8%)
  other arithmetic  42.7 us (8%)
  blocking collectives  31.3 us (6%)
  starting transfers between devices  20.6 us (4%)
  between operations  13.9 us (2%)
    reduce_scatter x1, waiting for transfers between devices, local(): lax.psum_scatter(jnp.concatenate([jnp.dot(left, gate_dense, preferred_ele...  198 us
    all_gather x1, waiting for transfers between devices, local(): all_rotated = lax.all_gather(rotated, 'dp', axis=0, tiled=True)  64.2 us
    all_gather x1, waiting for transfers between devices, local(): all_sign_bits = lax.all_gather(sign_bits, 'dp', axis=0, tiled=True)  46.8 us
    shift_right_arithmetic x6, local copies, waits for them, and re-layouts, dequant(): code_vals = jnp.bitwise_and(jnp.right_shift(whole, shifts), 15) - 8  39.4 us
    pmax x1, blocking collectives, local(): token_absmax = lax.pmax(local_peak, 'tensor')  31.3 us
    dot_general x1, matrix products, local(): jnp.dot(left, down_dense, preferred_element_type=jnp.float32)  29.2 us
    reduce_scatter x1, waiting for transfers between devices, local(): lax.psum_scatter(jnp.dot(left, down_dense, preferred_element_type=jnp.flo...  29.1 us
    shift_right_arithmetic x3, other arithmetic, dequant(): code_vals = jnp.bitwise_and(jnp.right_shift(whole, shifts), 15) - 8  12.8 us
  transfers between devices with their start and end apart: 9, of which 8 were waited for; matrix products, arithmetic and copies ran while one was open for 14% of the time, Pallas kernels for 0%

commit v1 on v0

v1 whole, which is shorter than its diff:
```python
import math

import jax
import jax.numpy as jnp
from jax import lax
from jax.experimental import pallas as pl
from jax.experimental.pallas import tpu as pltpu
from jax.sharding import PartitionSpec as P

FF = 53248
HB = 3328
NB = 13
NDP = 16
NT = 16
MESH = pl.DeviceIdType.MESH
BF = jnp.bfloat16
F32 = jnp.float32

LAG_Z = 2
LAG_H = 4
LAG_W = 5
LAG_G = 6
LAG_X = 8
LAG_S = 10
LAG_U = 5
TICKS = NB + LAG_S
NOUT = 2


def eo_column(p):
    return jnp.where(p < 128, 2 * p, 2 * (p - 128) + 1)


def one_hot(cond):
    return jnp.where(cond, 1.0, 0.0).astype(BF)


def body(tokens, gc, gs, uc, us, dc, ds, sb, out, peak,
         x, gcv, ucv, dcv, own, xr, zr, hs, w1r, v, g, sw, st, dw, racc, rot, es, er, pk, pr,
         gsv, usv, dsv, sbp, sbt, wb, perm_in, perm_h, perm_out, walsh,
         code_sem, dcode_sem, loc_sem, a_send, a_recv, sib_sem, s1_send, s1_recv, s2_send, s2_recv,
         x_send, x_recv, z_send, z_recv, w1_send, w1_recv, w2_send, w2_recv, g_send, g_recv,
         gx_send, gx_recv, e_send, e_recv, p_send, p_recv):
    d = lax.axis_index("dp")
    t = lax.axis_index("tensor")
    core = lax.rem(t, 2)
    s = lax.rem(t, 8)
    z = d // 2
    xh = lax.rem(d, 2)
    row = xh * 8 + z
    partner = z * 2 + (1 - xh)

    def place(dp):
        return lax.rem(dp, 2) * 8 + dp // 2

    def remote(src, dst, ssem, rsem, dp, tn):
        return pltpu.make_async_remote_copy(
            src_ref=src, dst_ref=dst, send_sem=ssem, recv_sem=rsem, device_id=(dp, tn), device_id_type=MESH)

    def wait_bytes(ref, sem):
        pltpu.make_async_copy(ref, ref, sem).wait()

    def code_copies(c):
        lanes = pl.ds(pl.multiple_of(c * 128, 128), 128)
        return (pltpu.make_async_copy(gc.at[:, lanes], gcv.at[c], code_sem.at[0, c]),
                pltpu.make_async_copy(uc.at[:, lanes], ucv.at[c], code_sem.at[1, c]))

    def start_codes(c, carry):
        for copy in code_copies(c):
            copy.start()
        return carry

    lax.fori_loop(0, NB, start_codes, 0)
    dcopy = pltpu.make_async_copy(dc, dcv, dcode_sem)
    dcopy.start()

    barrier = pltpu.get_barrier_semaphore()

    def greet(j, carry):
        pl.semaphore_signal(barrier, inc=1, device_id=(lax.rem(d + j, NDP), t), device_id_type=MESH)
        pl.semaphore_signal(barrier, inc=1, device_id=(d, lax.rem(t + j, NT)), device_id_type=MESH)
        return carry

    lax.fori_loop(1, NDP, greet, 0)

    sbp[...] = jnp.zeros_like(sbp)
    sbp[0:208, 0:208] = sb[...]
    sbt[...] = jnp.transpose(sbp[...]).reshape(16, 16, 256)

    @pl.when(s < 7)
    def _():
        for u in range(2):
            sw[2 * s + u, d] = sbt[2 * s + u].astype(jnp.int16)

    pl.semaphore_wait(barrier, 2 * (NDP - 1))

    def token_copy(dst_dp):
        lanes = pl.ds(pl.multiple_of(dst_dp * 1024 + core * 512, 512), 512)
        return tokens.at[:, lanes]

    def send_tokens(j, carry):
        to = lax.rem(d + j, NDP)
        remote(token_copy(to), x.at[core, row], a_send, a_recv, to, t).start()
        return carry

    lax.fori_loop(1, NDP, send_tokens, 0)
    mine = pltpu.make_async_copy(token_copy(d), x.at[core, row], loc_sem)
    mine.start()

    @pl.when(s < 7)
    def _():
        def send_words(j, carry):
            part = sw.at[pl.ds(2 * s, 2), d]
            remote(part, part, s1_send, s1_recv, lax.rem(d + j, NDP), t).start()
            return carry

        lax.fori_loop(1, NDP, send_words, 0)

    src = lax.broadcasted_iota(jnp.int32, (256, 256), 0)
    dst = lax.broadcasted_iota(jnp.int32, (256, 256), 1)
    perm_in[...] = one_hot(src == eo_column(dst))
    perm_out[...] = one_hot(dst == eo_column(src))
    perm_h[...] = one_hot(eo_column(src) == 16 * (dst & 15) + (dst >> 4))
    both = (src >> 4) & (dst >> 4)
    odd = (both ^ (both >> 1) ^ (both >> 2) ^ (both >> 3)) & 1
    walsh[...] = jnp.where((src & 15) == (dst & 15), jnp.where(odd == 1, -1.0, 1.0), 0.0).astype(BF)

    for b in range(NB):
        cols = slice(256 * b, 256 * b + 256)
        gsv[b] = jnp.dot(gs[:, cols], perm_in[...], preferred_element_type=F32)
        usv[b] = jnp.dot(us[:, cols], perm_in[...], preferred_element_type=F32)
    for n in range(4):
        cols = slice(256 * n, 256 * n + 256)
        dsv[:, cols] = jnp.dot(ds[:, cols], perm_in[...], preferred_element_type=F32)

    wait_bytes(x.at[core, pl.ds(0, NDP - 1)], a_recv)
    mine.wait()
    sib = remote(x.at[core], x.at[core], sib_sem.at[0], sib_sem.at[1], d, t + 1 - 2 * core)
    sib.start()
    sib.wait_recv()

    def nibbles(codes):
        whole = codes.astype(F32)
        high = jnp.floor(whole * 0.0625)
        return whole - 16.0 * high - 8.0, high - 8.0

    def gate_up(c):
        for copy in code_copies(c):
            copy.wait()
        for base, codes, scales in ((0, gcv, gsv), (256, ucv, usv)):
            for r in range(8):
                rows = slice(128 * r, 128 * r + 128)
                low, high = nibbles(codes[c, rows, :])
                sc = scales[c, r:r + 1, :]
                wb[rows, base:base + 128] = (low * sc[:, 0:128]).astype(BF)
                wb[rows, base + 128:base + 256] = (high * sc[:, 128:256]).astype(BF)
        part = jnp.dot(x[0].reshape(256, 512), wb[0:512, :], preferred_element_type=F32)
        part = part + jnp.dot(x[1].reshape(256, 512), wb[512:1024, :], preferred_element_type=F32)
        own[c] = part.astype(BF).reshape(16, 16, 512)
        remote(own.at[c, pl.ds((1 - xh) * 8, 8)], xr.at[c], x_send, x_recv.at[c], partner, t).start()

    def down_weights(b):
        @pl.when(b == 0)
        def _():
            dcopy.wait()

        for r in range(2):
            rows = pl.ds(pl.multiple_of(256 * b + 128 * r, 128), 128)
            low, high = nibbles(dcv[rows, :])
            sc = dsv[pl.ds(2 * b + r, 1), :]
            for n in range(4):
                words = slice(128 * n, 128 * n + 128)
                dw[rows, 256 * n:256 * n + 128] = (low[:, words] * sc[:, 256 * n:256 * n + 128]).astype(BF)
                dw[rows, 256 * n + 128:256 * n + 256] = (high[:, words] * sc[:, 256 * n + 128:256 * n + 256]).astype(BF)

    def share_words():
        @pl.when(s < 7)
        def _():
            wait_bytes(sw.at[pl.ds(0, 2), pl.ds(0, NDP - 1)], s1_recv)

            def send(j, carry):
                to = t - s + lax.rem(s + j, 8)
                part = sw.at[pl.ds(2 * s, 2)]
                remote(part, part, s2_send, s2_recv.at[s], d, to).start()
                return carry

            lax.fori_loop(1, 8, send, 0)

    def wait_words():
        for q in range(7):
            @pl.when(s != q)
            def _():
                wait_bytes(sw.at[pl.ds(2 * q, 2)], s2_recv.at[q])

    def unpack(b):
        words = jnp.concatenate([sw[b, q].astype(jnp.int32)[:, 0:208] for q in range(NDP)], axis=1)
        for k in range(16):
            st[b, 16 * k:16 * k + 16, :] = jnp.where((words & (1 << k)) == 0, 1.0, -1.0).astype(BF)

    def z_phase(c):
        wait_bytes(xr.at[c], x_recv.at[c])
        half = pl.ds(xh * 8, 8)
        own[c, half] = (own[c, half].astype(F32) + xr[c].astype(F32)).astype(BF)

        def send(j, carry):
            zz = lax.rem(z + j, 8)
            remote(own.at[c, xh * 8 + zz], zr.at[c, j - 1], z_send, z_recv.at[c], zz * 2 + xh, t).start()
            return carry

        lax.fori_loop(1, 8, send, 0)

    def hidden(c):
        wait_bytes(zr.at[c], z_recv.at[c])
        total = own[c, row].astype(F32)
        for j in range(7):
            total = total + zr[c, j].astype(F32)
        gate, up = total[:, 0:256], total[:, 256:512]
        hs[c] = (gate / (1.0 + jnp.exp(-gate)) * up).astype(BF)

        @pl.when(t == c)
        def _():
            w1r[t] = hs[c]

        @pl.when(t != c)
        def _():
            remote(hs.at[c], w1r.at[t], w1_send, w1_recv, d, c).start()

    def mix(c):
        @pl.when(t == c)
        def _():
            wait_bytes(w1r.at[pl.ds(0, NT - 1)], w1_recv)
            turned = jnp.dot(w1r[...].reshape(256, 256), perm_h[...], preferred_element_type=F32).astype(BF)
            mixed = jnp.dot(walsh[...], turned, preferred_element_type=F32) * (1.0 / math.sqrt(FF))
            v[...] = mixed.astype(BF).reshape(16, 16, 256)
            g[c, row] = v[t]

            def send(j, carry):
                to = lax.rem(t + j, NT)
                remote(v.at[to], g.at[c, row], w2_send, w2_recv.at[c], d, to).start()
                return carry

            lax.fori_loop(1, NT, send, 0)

    def gather_z(b):
        @pl.when(t != b)
        def _():
            wait_bytes(g.at[b, row], w2_recv.at[b])

        def send(j, carry):
            zz = lax.rem(z + j, 8)
            remote(g.at[b, row], g.at[b, row], g_send, g_recv.at[b], zz * 2 + xh, t).start()
            return carry

        lax.fori_loop(1, 8, send, 0)

    def gather_x(b):
        wait_bytes(g.at[b, pl.ds(xh * 8, 7)], g_recv.at[b])
        half = g.at[b, pl.ds(xh * 8, 8)]
        remote(half, half, gx_send, gx_recv.at[b], partner, t).start()

    def turn(b):
        wait_bytes(g.at[b, pl.ds((1 - xh) * 8, 8)], gx_recv.at[b])
        left = g[b].reshape(256, 256)
        for n in range(NB):
            cols = slice(256 * n, 256 * n + 256)
            racc[:, cols] += jnp.dot(left, st[b, :, cols], preferred_element_type=F32)

    def during(i, lag, stage):
        @pl.when((i >= lag) & (i < NB + lag))
        def _():
            stage(i - lag)

    racc[...] = jnp.zeros_like(racc)

    def tick(i, carry):
        during(i, 0, gate_up)
        during(i, LAG_Z, z_phase)
        during(i, LAG_H, hidden)
        during(i, LAG_W, mix)
        during(i, LAG_G, gather_z)
        during(i, LAG_X, gather_x)

        @pl.when(i == 1)
        def _():
            share_words()

        during(i, 1, down_weights)

        @pl.when(i == LAG_U)
        def _():
            wait_words()

        during(i, LAG_U, unpack)
        during(i, LAG_S, turn)
        return carry

    lax.fori_loop(0, TICKS, tick, 0)

    rot[...] = racc[...].astype(BF).reshape(16, 16, HB)
    top = jnp.max(jnp.abs(rot[row].astype(F32)), axis=1, keepdims=True)
    pk[...] = jnp.broadcast_to(top, (16, 128))
    pr[t] = pk[...]

    def send_peak(j, carry):
        remote(pk, pr.at[t], p_send, p_recv, d, lax.rem(t + j, NT)).start()
        return carry

    lax.fori_loop(1, NT, send_peak, 0)

    width = 1024 // NOUT
    for n in range(NOUT):
        cols = slice(width * n, width * n + width)
        part = jnp.dot(rot[...].reshape(256, HB), dw[:, cols], preferred_element_type=F32)
        es[n] = part.astype(BF).reshape(16, 16, width)
        er[n, t] = es[n, place(t)]

        def send_out(j, carry, n=n):
            to = lax.rem(t + j, NT)
            remote(es.at[n, place(to)], er.at[n, t], e_send.at[n], e_recv.at[n], d, to).start()
            return carry

        lax.fori_loop(1, NT, send_out, 0)

    wait_bytes(pr.at[pl.ds(0, NT - 1)], p_recv)
    high = pr[0]
    for q in range(1, NT):
        high = jnp.maximum(high, pr[q])
    peak[...] = jnp.transpose(high)[0:1, :]

    for n in range(NOUT):
        wait_bytes(er.at[n, pl.ds(0, NT - 1)], e_recv.at[n])
        total = er[n, 0].astype(F32)
        for q in range(1, NT):
            total = total + er[n, q].astype(F32)
        total = total.astype(BF)
        for m in range(width // 256):
            lo = width * n + 256 * m
            out[:, lo:lo + 256] = jnp.dot(
                total[:, 256 * m:256 * m + 256], perm_out[...], preferred_element_type=F32).astype(BF)

    wait_bytes(x.at[core, pl.ds(0, NDP - 1)], a_send)
    sib.wait_send()

    @pl.when(s < 7)
    def _():
        wait_bytes(sw.at[pl.ds(0, 2), pl.ds(0, NDP - 1)], s1_send)
        wait_bytes(sw, s2_send)

    wait_bytes(xr, x_send)
    wait_bytes(zr, z_send)

    @pl.when(t < NB)
    def _():
        wait_bytes(hs.at[pl.ds(0, NB - 1)], w1_send)
        wait_bytes(v.at[pl.ds(0, NT - 1)], w2_send)

    @pl.when(t >= NB)
    def _():
        wait_bytes(hs, w1_send)

    wait_bytes(g.at[:, pl.ds(0, 7)], g_send)
    wait_bytes(g.at[:, pl.ds(0, 8)], gx_send)
    for n in range(NOUT):
        wait_bytes(es.at[n, pl.ds(0, NT - 1)], e_send.at[n])
    wait_bytes(pr.at[pl.ds(0, NT - 1)], p_send)


def local(tokens, gc, gs, uc, us, dc, ds, sb):
    dma = pltpu.SemaphoreType.DMA
    vm = pltpu.VMEM
    any_spec = pl.BlockSpec(memory_space=pl.ANY)
    vm_spec = pl.BlockSpec(memory_space=pltpu.VMEM)
    width = 1024 // NOUT
    out, peak = pl.pallas_call(
        body,
        out_shape=(jax.ShapeDtypeStruct((16, 1024), BF), jax.ShapeDtypeStruct((1, 16), F32)),
        in_specs=[any_spec, any_spec, vm_spec, any_spec, vm_spec, any_spec, vm_spec, vm_spec],
        out_specs=(vm_spec, vm_spec),
        scratch_shapes=[
            vm((2, 16, 16, 512), BF),
            vm((NB, 1024, 128), BF),
            vm((NB, 1024, 128), BF),
            vm((HB, 512), BF),
            vm((NB, 16, 16, 512), BF),
            vm((NB, 8, 16, 512), BF),
            vm((NB, 7, 16, 512), BF),
            vm((NB, 16, 256), BF),
            vm((16, 16, 256), BF),
            vm((16, 16, 256), BF),
            vm((NB, 16, 16, 256), BF),
            vm((14, 16, 16, 256), jnp.int16),
            vm((NB, 256, HB), BF),
            vm((HB, 1024), BF),
            vm((256, HB), F32),
            vm((16, 16, HB), BF),
            vm((NOUT, 16, 16, width), BF),
            vm((NOUT, 16, 16, width), BF),
            vm((16, 128), F32),
            vm((16, 16, 128), F32),
            vm((NB, 8, 256), F32),
            vm((NB, 8, 256), F32),
            vm((26, 1024), F32),
            vm((256, 256), jnp.int32),
            vm((16, 16, 256), jnp.int32),
            vm((1024, 512), BF),
            vm((256, 256), BF),
            vm((256, 256), BF),
            vm((256, 256), BF),
            vm((256, 256), BF),
            dma((2, NB)), dma, dma, dma, dma, dma((2,)), dma, dma, dma, dma((8,)),
            dma, dma((NB,)), dma, dma((NB,)), dma, dma, dma, dma((NB,)), dma, dma((NB,)),
            dma, dma((NB,)), dma((NOUT,)), dma((NOUT,)), dma, dma,
        ],
        compiler_params=pltpu.CompilerParams(
            collective_id=0, has_side_effects=True, vmem_limit_bytes=63 * 1024 * 1024),
    )(tokens, gc, gs, uc, us, dc, ds, sb)
    return out, peak.reshape(16)


def solution(mesh):
    return jax.shard_map(
        local,
        mesh=mesh,
        in_specs=(
            P("dp", None),
            P("dp", "tensor"),
            P("dp", "tensor"),
            P("dp", "tensor"),
            P("dp", "tensor"),
            P("tensor", "dp"),
            P("tensor", "dp"),
            P("dp", None),
        ),
        out_specs=(P("tensor", "dp"), P("dp")),
        check_vma=False,
    )
```

time: 563 us -> 127 us (0.23)
  waiting for transfers between devices: 349 us -> 0 us
  Pallas kernels: 0 us -> 124 us
  local copies, waits for them, and re-layouts: 55.7 us -> 2.55 us
  matrix products: 47.1 us -> 0 us
  other arithmetic: 42.7 us -> 0 us
  blocking collectives: 31.3 us -> 0 us
  starting transfers between devices: 20.6 us -> 0 us
  between operations: 13.9 us -> 0.64 us
    reduce_scatter x2 -> x0, waiting for transfers between devices: 227 us -> none  [the longest x1 198 us: local(): lax.psum_scatter(jnp.concatenate([jnp.dot(left, gate_dense, preferred_ele...]
    pallas_call x0 -> x1, Pallas kernels: none -> 124 us  [local(): pl.pallas_call(body, out_shape=(jax.ShapeDtypeStruct((16, 1024), BF), jax...]
    all_gather x2 -> x0, waiting for transfers between devices: 111 us -> none  [the longest x1 64.2 us: local(): all_rotated = lax.all_gather(rotated, 'dp', axis=0, tiled=True)]
    dot_general x4 -> x0, matrix products: 47.1 us -> none  [the longest x1 29.2 us: local(): jnp.dot(left, down_dense, preferred_element_type=jnp.float32)]
    shift_right_arithmetic x8 -> x0, local copies, waits for them, and re-layouts: 39.5 us -> none  [the longest x6 39.4 us: dequant(): code_vals = jnp.bitwise_and(jnp.right_shift(whole, shifts), 15) - 8]
    pmax x1 -> x0, blocking collectives: 31.3 us -> none  [local(): token_absmax = lax.pmax(local_peak, 'tensor')]
    convert_element_type x6 -> x0, other arithmetic: 27.8 us -> none  [the longest x1 11 us: dequant(): values = (code_vals.astype(jnp.float32) * scale_grid).astype(jnp.bfloat16)]
    shift_right_arithmetic x3 -> x0, other arithmetic: 12.8 us -> none  [dequant(): code_vals = jnp.bitwise_and(jnp.right_shift(whole, shifts), 15) - 8]
  transfers between devices with their start and end apart: 9 -> 0, of which waited for: 8 -> 0; matrix products, arithmetic and copies ran while one was open for 14% -> 0% of each run, Pallas kernels for 0% -> 0%
where the time goes in v1:
time: 127 us
  Pallas kernels  124 us (98%)
  local copies, waits for them, and re-layouts  2.55 us (2%)
    pallas_call x1, Pallas kernels, local(): pl.pallas_call(body, out_shape=(jax.ShapeDtypeStruct((16, 1024), BF), jax...  124 us
    unnamed x2, local copies, waits for them, and re-layouts  2.55 us

profile of v1, /device:TPU:1, one launch (start us, length us, event | category | flops | bytes accessed | tf_op | source)
XLA Modules:
  0.0 127.2 jit_solution(10538002754825701299)
XLA Ops:
  0.6 124.0 %shard_map.95 = (bf16[16,1024]{1,0:T(8,128)(2,1)}, f32[1,16]{1,0:T(1,128)}) custom-call(bf16[16,16384]{1,0:T(8,128)(2,1)} %tokens.1, bf16[1024,1664]{1,0:T(8,128)(2,1)} %gc.1, bf16[8,3328]{1,0:T(8,128)(2,1)} %gs.1, bf16[1024,1664]{1,0:T(8,128)(2,1)} %uc.1, bf16[8,3328]{1,0:T(8,128)(2,1)} %us.1, bf16[3328,512]{1,0:T(8,128)(2,1)} %dc.1, bf16[26,1024]{1,0:T(8,128)(2,1)} %ds.1, ...), custom_call_target="tpu_custom_call" | custom-call | tf_op jit(solution)/shard_map/pallas_call | solution.py:374
  124.6 1.4 %copy.12 = bf16[16,1024]{1,0:T(8,128)(2,1)} copy(bf16[16,1024]{1,0:T(8,128)(2,1)} %get-tuple-element.8) | data formatting | bytes 65536
  126.0 1.2 copy.13

commit v2 on v1

--- a/solution.py
+++ b/solution.py
@@ -16,14 +16,19 @@
 BF = jnp.bfloat16
 F32 = jnp.float32
 
-LAG_Z = 2
-LAG_H = 4
-LAG_W = 5
-LAG_G = 6
-LAG_X = 8
-LAG_S = 10
-LAG_U = 5
-TICKS = NB + LAG_S
+NE = 9
+ZEND = 5
+NZF = (ZEND + 2) // 3
+LAG_Z = (2, 2)
+LAG_H = (6, 4)
+LAG_W = (7, 5)
+LAG_G = (8, 6)
+LAG_X = (10, 8)
+LAG_S = (12, 10)
+TICKS = max(NE + LAG_S[0], NB + LAG_S[1])
+T_SHARE = 2
+T_SIBLING = 8
+T_WORDS = min(LAG_S[0], NE + LAG_S[1])
 NOUT = 2
 
 
@@ -36,22 +41,20 @@
 
 
 def body(tokens, gc, gs, uc, us, dc, ds, sb, out, peak,
-         x, gcv, ucv, dcv, own, xr, zr, hs, w1r, v, g, sw, st, dw, racc, rot, es, er, pk, pr,
+         x, gcv, ucv, dcv, own, xr, zr, zr2, xr2, hs, w1r, v, g, sw, st, dw, racc, rot, es, er, pk, pr,
          gsv, usv, dsv, sbp, sbt, wb, perm_in, perm_h, perm_out, walsh,
          code_sem, dcode_sem, loc_sem, a_send, a_recv, sib_sem, s1_send, s1_recv, s2_send, s2_recv,
-         x_send, x_recv, z_send, z_recv, w1_send, w1_recv, w2_send, w2_recv, g_send, g_recv,
+         s3_sem, x_send, x_recv, x2_send, x2_recv, z_send, z_recv, zz_send, zz_recv, w1_send, w1_recv, w2_send, w2_recv, g_send, g_recv,
          gx_send, gx_recv, e_send, e_recv, p_send, p_recv):
     d = lax.axis_index("dp")
     t = lax.axis_index("tensor")
     core = lax.rem(t, 2)
-    s = lax.rem(t, 8)
+    y = lax.rem(t // 2, 4)
+    s = core * 4 + y
     z = d // 2
     xh = lax.rem(d, 2)
-    row = xh * 8 + z
     partner = z * 2 + (1 - xh)
-
-    def place(dp):
-        return lax.rem(dp, 2) * 8 + dp // 2
+    sibling = t + 1 - 2 * core
 
     def remote(src, dst, ssem, rsem, dp, tn):
         return pltpu.make_async_remote_copy(
@@ -59,6 +62,15 @@
 
     def wait_bytes(ref, sem):
         pltpu.make_async_copy(ref, ref, sem).wait()
+
+    barrier = pltpu.get_barrier_semaphore()
+
+    def greet(j, carry):
+        pl.semaphore_signal(barrier, inc=1, device_id=(lax.rem(d + j, NDP), t), device_id_type=MESH)
+        pl.semaphore_signal(barrier, inc=1, device_id=(d, lax.rem(t + j, NT)), device_id_type=MESH)
+        return carry
+
+    lax.fori_loop(1, NDP, greet, 0)
 
     def code_copies(c):
         lanes = pl.ds(pl.multiple_of(c * 128, 128), 128)
@@ -74,15 +86,6 @@
     dcopy = pltpu.make_async_copy(dc, dcv, dcode_sem)
     dcopy.start()
 
-    barrier = pltpu.get_barrier_semaphore()
-
-    def greet(j, carry):
-        pl.semaphore_signal(barrier, inc=1, device_id=(lax.rem(d + j, NDP), t), device_id_type=MESH)
-        pl.semaphore_signal(barrier, inc=1, device_id=(d, lax.rem(t + j, NT)), device_id_type=MESH)
-        return carry
-
-    lax.fori_loop(1, NDP, greet, 0)
-
     sbp[...] = jnp.zeros_like(sbp)
     sbp[0:208, 0:208] = sb[...]
     sbt[...] = jnp.transpose(sbp[...]).reshape(16, 16, 256)
@@ -100,11 +103,11 @@
 
     def send_tokens(j, carry):
         to = lax.rem(d + j, NDP)
-        remote(token_copy(to), x.at[core, row], a_send, a_recv, to, t).start()
+        remote(token_copy(to), x.at[core, d], a_send, a_recv, to, t).start()
         return carry
 
     lax.fori_loop(1, NDP, send_tokens, 0)
-    mine = pltpu.make_async_copy(token_copy(d), x.at[core, row], loc_sem)
+    mine = pltpu.make_async_copy(token_copy(d), x.at[core, d], loc_sem)
     mine.start()
 
     @pl.when(s < 7)
@@ -135,7 +138,7 @@
 
     wait_bytes(x.at[core, pl.ds(0, NDP - 1)], a_recv)
     mine.wait()
-    sib = remote(x.at[core], x.at[core], sib_sem.at[0], sib_sem.at[1], d, t + 1 - 2 * core)
+    sib = remote(x.at[core], x.at[core], sib_sem.at[0], sib_sem.at[1], d, sibling)
     sib.start()
     sib.wait_recv()
 
@@ -156,8 +159,15 @@
                 wb[rows, base + 128:base + 256] = (high * sc[:, 128:256]).astype(BF)
         part = jnp.dot(x[0].reshape(256, 512), wb[0:512, :], preferred_element_type=F32)
         part = part + jnp.dot(x[1].reshape(256, 512), wb[512:1024, :], preferred_element_type=F32)
-        own[c] = part.astype(BF).reshape(16, 16, 512)
-        remote(own.at[c, pl.ds((1 - xh) * 8, 8)], xr.at[c], x_send, x_recv.at[c], partner, t).start()
+        own[c] = part.astype(BF).reshape(8, 2, 16, 512)
+
+        @pl.when(z_first(c))
+        def _():
+            chain(c, 1, True)
+
+        @pl.when(jnp.logical_not(z_first(c)))
+        def _():
+            remote(own.at[c, :, 1 - xh], xr.at[c], x_send, x_recv.at[c], partner, t).start()
 
     def down_weights(b):
         @pl.when(b == 0)
@@ -179,44 +189,124 @@
             wait_bytes(sw.at[pl.ds(0, 2), pl.ds(0, NDP - 1)], s1_recv)
 
             def send(j, carry):
-                to = t - s + lax.rem(s + j, 8)
+                to = t + 2 * (lax.rem(y + j, 4) - y)
                 part = sw.at[pl.ds(2 * s, 2)]
-                remote(part, part, s2_send, s2_recv.at[s], d, to).start()
+                remote(part, part, s2_send, s2_recv.at[y], d, to).start()
                 return carry
 
-            lax.fori_loop(1, 8, send, 0)
-
-    def wait_words():
-        for q in range(7):
-            @pl.when(s != q)
+            lax.fori_loop(1, 4, send, 0)
+
+    def words_to_sibling():
+        for q in range(4):
+            @pl.when((y != q) & (core * 4 + q < 7))
             def _():
                 wait_bytes(sw.at[pl.ds(2 * q, 2)], s2_recv.at[q])
+
+        @pl.when(core == 0)
+        def _():
+            remote(sw.at[pl.ds(0, 8)], sw.at[pl.ds(0, 8)], s3_sem.at[0], s3_sem.at[1], d, sibling).start()
+
+        @pl.when(core == 1)
+        def _():
+            remote(sw.at[pl.ds(8, 6)], sw.at[pl.ds(8, 6)], s3_sem.at[0], s3_sem.at[1], d, sibling).start()
+
+    def words_of(which, sem):
+        @pl.when(core == which)
+        def _():
+            wait_bytes(sw.at[pl.ds(0, 8)], sem)
+
+        @pl.when(core != which)
+        def _():
+            wait_bytes(sw.at[pl.ds(8, 6)], sem)
 
     def unpack(b):
         words = jnp.concatenate([sw[b, q].astype(jnp.int32)[:, 0:208] for q in range(NDP)], axis=1)
         for k in range(16):
-            st[b, 16 * k:16 * k + 16, :] = jnp.where((words & (1 << k)) == 0, 1.0, -1.0).astype(BF)
-
-    def z_phase(c):
+            st[16 * k:16 * k + 16, :] = jnp.where((words & (1 << k)) == 0, 1.0, -1.0).astype(BF)
+
+    def z_first(c):
+        return (lax.rem(c, 3) == 0) & (c < ZEND)
+
+    def chain(c, step, first):
+        sign = 1 - 2 * lax.rem(c, 2)
+        buf, ss, rs, m = (zr2, zz_send, zz_recv, c // 3) if first else (zr, z_send, z_recv, c)
+        for way, base, steps in ((1, 0, 4), (-1, 4, 3)):
+            if step > steps:
+                continue
+            owner = lax.rem(z + way * sign * (steps + 1 - step) + 8, 8)
+            term = own.at[c, owner] if first else own.at[c, owner, xh]
+            if step > 1:
+                src = buf.at[m, base + step - 2]
+                wait_bytes(src, rs.at[m, base + step - 2])
+                src[...] = (src[...].astype(F32) + term[...].astype(F32)).astype(BF)
+            else:
+                src = term
+            to = lax.rem(z + way * sign + 8, 8) * 2 + xh
+            remote(src, buf.at[m, base + step - 1], ss, rs.at[m, base + step - 1], to, t).start()
+
+    def z_total(c, first):
+        buf, rs, m = (zr2, zz_recv, c // 3) if first else (zr, z_recv, c)
+        term = own[c, z] if first else own[c, z, xh]
+        wait_bytes(buf.at[m, 3], rs.at[m, 3])
+        wait_bytes(buf.at[m, 6], rs.at[m, 6])
+        return term.astype(F32) + buf[m, 3].astype(F32) + buf[m, 6].astype(F32)
+
+    def z_step(step):
+        def stage(c):
+            @pl.when(z_first(c))
+            def _():
+                if step < 4:
+                    chain(c, step + 1, True)
+                else:
+                    own[c, z] = z_total(c, True).astype(BF)
+                    remote(own.at[c, z, 1 - xh], xr2.at[c // 3], x2_send, x2_recv.at[c // 3], partner, t).start()
+
+            @pl.when(jnp.logical_not(z_first(c)))
+            def _():
+                if step == 1:
+                    add_partner(c)
+                chain(c, step, False)
+        return stage
+
+    def add_partner(c):
         wait_bytes(xr.at[c], x_recv.at[c])
-        half = pl.ds(xh * 8, 8)
-        own[c, half] = (own[c, half].astype(F32) + xr[c].astype(F32)).astype(BF)
+        own[c, :, xh] = (own[c, :, xh].astype(F32) + xr[c].astype(F32)).astype(BF)
+
+    def z_direct(c):
+        add_partner(c)
 
         def send(j, carry):
             zz = lax.rem(z + j, 8)
-            remote(own.at[c, xh * 8 + zz], zr.at[c, j - 1], z_send, z_recv.at[c], zz * 2 + xh, t).start()
+            remote(own.at[c, zz, xh], zr.at[c, j - 1], z_send, z_recv.at[c, 0], zz * 2 + xh, t).start()
             return carry
 
         lax.fori_loop(1, 8, send, 0)
 
-    def hidden(c):
-        wait_bytes(zr.at[c], z_recv.at[c])
-        total = own[c, row].astype(F32)
+    def activate(c, total):
+        gate, up = total[:, 0:256], total[:, 256:512]
+        hs[c] = (gate / (1.0 + jnp.exp(-gate)) * up).astype(BF)
+
+    def hidden_chain(c):
+        @pl.when(z_first(c))
+        def _():
+            wait_bytes(xr2.at[c // 3], x2_recv.at[c // 3])
+            activate(c, own[c, z, xh].astype(F32) + xr2[c // 3].astype(F32))
+
+        @pl.when(jnp.logical_not(z_first(c)))
+        def _():
+            activate(c, z_total(c, False))
+
+        send_hidden(c)
+
+    def hidden_direct(c):
+        wait_bytes(zr.at[c], z_recv.at[c, 0])
+        total = own[c, z, xh].astype(F32)
         for j in range(7):
             total = total + zr[c, j].astype(F32)
-        gate, up = total[:, 0:256], total[:, 256:512]
-        hs[c] = (gate / (1.0 + jnp.exp(-gate)) * up).astype(BF)
-
+        activate(c, total)
+        send_hidden(c)
+
+    def send_hidden(c):
         @pl.when(t == c)
         def _():
             w1r[t] = hs[c]
@@ -232,11 +322,11 @@
             turned = jnp.dot(w1r[...].reshape(256, 256), perm_h[...], preferred_element_type=F32).astype(BF)
             mixed = jnp.dot(walsh[...], turned, preferred_element_type=F32) * (1.0 / math.sqrt(FF))
             v[...] = mixed.astype(BF).reshape(16, 16, 256)
-            g[c, row] = v[t]
+            g[c, z, xh] = v[t]
 
             def send(j, carry):
                 to = lax.rem(t + j, NT)
-                remote(v.at[to], g.at[c, row], w2_send, w2_recv.at[c], d, to).start()
+                remote(v.at[to], g.at[c, z, xh], w2_send, w2_recv.at[c], d, to).start()
                 return carry
 
             lax.fori_loop(1, NT, send, 0)
@@ -244,60 +334,76 @@
     def gather_z(b):
         @pl.when(t != b)
         def _():
-            wait_bytes(g.at[b, row], w2_recv.at[b])
+            wait_bytes(g.at[b, z, xh], w2_recv.at[b])
 
         def send(j, carry):
             zz = lax.rem(z + j, 8)
-            remote(g.at[b, row], g.at[b, row], g_send, g_recv.at[b], zz * 2 + xh, t).start()
+            remote(g.at[b, z, xh], g.at[b, z, xh], g_send, g_recv.at[b], zz * 2 + xh, t).start()
             return carry
 
         lax.fori_loop(1, 8, send, 0)
 
     def gather_x(b):
-        wait_bytes(g.at[b, pl.ds(xh * 8, 7)], g_recv.at[b])
-        half = g.at[b, pl.ds(xh * 8, 8)]
+        wait_bytes(g.at[b, pl.ds(0, 7), xh], g_recv.at[b])
+        half = g.at[b, :, xh]
         remote(half, half, gx_send, gx_recv.at[b], partner, t).start()
 
     def turn(b):
-        wait_bytes(g.at[b, pl.ds((1 - xh) * 8, 8)], gx_recv.at[b])
+        wait_bytes(g.at[b, :, 1 - xh], gx_recv.at[b])
+        unpack(b)
         left = g[b].reshape(256, 256)
         for n in range(NB):
             cols = slice(256 * n, 256 * n + 256)
-            racc[:, cols] += jnp.dot(left, st[b, :, cols], preferred_element_type=F32)
-
-    def during(i, lag, stage):
-        @pl.when((i >= lag) & (i < NB + lag))
+            racc[:, cols] += jnp.dot(left, st[:, cols], preferred_element_type=F32)
+
+    def during(i, lag, stage, first, last):
+        @pl.when((i >= first + lag) & (i < last + lag))
         def _():
             stage(i - lag)
 
+    def each(i, lags, stage):
+        if lags[0] == lags[1]:
+            during(i, lags[0], stage, 0, NB)
+        else:
+            during(i, lags[0], stage, 0, NE)
+            during(i, lags[1], stage, NE, NB)
+
     racc[...] = jnp.zeros_like(racc)
 
     def tick(i, carry):
-        during(i, 0, gate_up)
-        during(i, LAG_Z, z_phase)
-        during(i, LAG_H, hidden)
-        during(i, LAG_W, mix)
-        during(i, LAG_G, gather_z)
-        during(i, LAG_X, gather_x)
-
-        @pl.when(i == 1)
+        during(i, 0, gate_up, 0, NB)
+        if NE:
+            for step in range(1, 5):
+                during(i, LAG_Z[0] + step - 1, z_step(step), 0, NE)
+        during(i, LAG_Z[1], z_direct, NE, NB)
+        if NE:
+            during(i, LAG_H[0], hidden_chain, 0, NE)
+        during(i, LAG_H[1], hidden_direct, NE, NB)
+        each(i, LAG_W, mix)
+        each(i, LAG_G, gather_z)
+        each(i, LAG_X, gather_x)
+
+        @pl.when(i == T_SHARE)
         def _():
             share_words()
 
-        during(i, 1, down_weights)
-
-        @pl.when(i == LAG_U)
-        def _():
-            wait_words()
-
-        during(i, LAG_U, unpack)
-        during(i, LAG_S, turn)
+        during(i, 1, down_weights, 0, NB)
+
+        @pl.when(i == T_SIBLING)
+        def _():
+            words_to_sibling()
+
+        @pl.when(i == T_WORDS)
+        def _():
+            words_of(1, s3_sem.at[1])
+
+        each(i, LAG_S, turn)
         return carry
 
     lax.fori_loop(0, TICKS, tick, 0)
 
     rot[...] = racc[...].astype(BF).reshape(16, 16, HB)
-    top = jnp.max(jnp.abs(rot[row].astype(F32)), axis=1, keepdims=True)
+    top = jnp.max(jnp.abs(rot[d].astype(F32)), axis=1, keepdims=True)
     pk[...] = jnp.broadcast_to(top, (16, 128))
     pr[t] = pk[...]
 
@@ -312,11 +418,11 @@
         cols = slice(width * n, width * n + width)
         part = jnp.dot(rot[...].reshape(256, HB), dw[:, cols], preferred_element_type=F32)
         es[n] = part.astype(BF).reshape(16, 16, width)
-        er[n, t] = es[n, place(t)]
+        er[n, t] = es[n, t]
 
         def send_out(j, carry, n=n):
             to = lax.rem(t + j, NT)
-            remote(es.at[n, place(to)], er.at[n, t], e_send.at[n], e_recv.at[n], d, to).start()
+            remote(es.at[n, to], er.at[n, t], e_send.at[n], e_recv.at[n], d, to).start()
             return carry
 
         lax.fori_loop(1, NT, send_out, 0)
@@ -344,10 +450,14 @@
     @pl.when(s < 7)
     def _():
         wait_bytes(sw.at[pl.ds(0, 2), pl.ds(0, NDP - 1)], s1_send)
-        wait_bytes(sw, s2_send)
-
-    wait_bytes(xr, x_send)
-    wait_bytes(zr, z_send)
+        wait_bytes(sw.at[pl.ds(0, 6)], s2_send)
+
+    words_of(0, s3_sem.at[0])
+    wait_bytes(xr.at[pl.ds(0, NB - NZF)], x_send)
+    wait_bytes(zr.at[pl.ds(0, NB - NZF)], z_send)
+    if NZF:
+        wait_bytes(xr2, x2_send)
+        wait_bytes(zr2, zz_send)
 
     @pl.when(t < NB)
     def _():
@@ -358,8 +468,8 @@
     def _():
         wait_bytes(hs, w1_send)
 
-    wait_bytes(g.at[:, pl.ds(0, 7)], g_send)
-    wait_bytes(g.at[:, pl.ds(0, 8)], gx_send)
+    wait_bytes(g.at[:, pl.ds(0, 7), 0], g_send)
+    wait_bytes(g.at[:, :, 0], gx_send)
     for n in range(NOUT):
         wait_bytes(es.at[n, pl.ds(0, NT - 1)], e_send.at[n])
     wait_bytes(pr.at[pl.ds(0, NT - 1)], p_send)
@@ -381,15 +491,17 @@
             vm((NB, 1024, 128), BF),
             vm((NB, 1024, 128), BF),
             vm((HB, 512), BF),
-            vm((NB, 16, 16, 512), BF),
+            vm((NB, 8, 2, 16, 512), BF),
             vm((NB, 8, 16, 512), BF),
             vm((NB, 7, 16, 512), BF),
+            vm((max(NZF, 1), 7, 2, 16, 512), BF),
+            vm((max(NZF, 1), 16, 512), BF),
             vm((NB, 16, 256), BF),
             vm((16, 16, 256), BF),
             vm((16, 16, 256), BF),
-            vm((NB, 16, 16, 256), BF),
+            vm((NB, 8, 2, 16, 256), BF),
             vm((14, 16, 16, 256), jnp.int16),
-            vm((NB, 256, HB), BF),
+            vm((256, HB), BF),
             vm((HB, 1024), BF),
             vm((256, HB), F32),
             vm((16, 16, HB), BF),
@@ -407,13 +519,25 @@
             vm((256, 256), BF),
             vm((256, 256), BF),
             vm((256, 256), BF),
-            dma((2, NB)), dma, dma, dma, dma, dma((2,)), dma, dma, dma, dma((8,)),
-            dma, dma((NB,)), dma, dma((NB,)), dma, dma, dma, dma((NB,)), dma, dma((NB,)),
+            dma((2, NB)), dma, dma, dma, dma, dma((2,)), dma, dma, dma, dma((4,)),
+            dma((2,)), dma, dma((NB,)), dma, dma((max(NZF, 1),)), dma, dma((NB, 7)), dma, dma((max(NZF, 1), 7)), dma, dma, dma, dma((NB,)), dma, dma((NB,)),
             dma, dma((NB,)), dma((NOUT,)), dma((NOUT,)), dma, dma,
         ],
         compiler_params=pltpu.CompilerParams(
             collective_id=0, has_side_effects=True, vmem_limit_bytes=63 * 1024 * 1024),
     )(tokens, gc, gs, uc, us, dc, ds, sb)
+
+    def hand_on(a, b, c, e, sems):
+        copies = (pltpu.make_async_copy(a, c, sems.at[0]), pltpu.make_async_copy(b, e, sems.at[1]))
+        for copy in copies:
+            copy.start()
+        for copy in copies:
+            copy.wait()
+
+    out, peak = pl.pallas_call(
+        hand_on, out_shape=(jax.ShapeDtypeStruct((16, 1024), BF), jax.ShapeDtypeStruct((1, 16), F32)),
+        in_specs=[any_spec, any_spec], out_specs=(any_spec, any_spec), scratch_shapes=[dma((2,))],
+        compiler_params=pltpu.CompilerParams(vmem_limit_bytes=63 * 1024 * 1024))(out, peak)
     return out, peak.reshape(16)
 
 

time: 127 us -> 112 us (0.88)
  Pallas kernels: 124 us -> 111 us
  local copies, waits for them, and re-layouts: 2.55 us -> 0 us
    pallas_call x1, Pallas kernels: 124 us -> 109 us  [local(): pl.pallas_call(body, out_shape=(jax.ShapeDtypeStruct((16, 1024), BF), jax...]
    unnamed x2 -> x0, local copies, waits for them, and re-layouts: 2.55 us -> none
    pallas_call x0 -> x1, Pallas kernels: none -> 2.13 us  [local(): pl.pallas_call(hand_on, out_shape=(jax.ShapeDtypeStruct((16, 1024), BF),...]
where the time goes in v2:
time: 112 us
  Pallas kernels  111 us (99%)
    pallas_call x1, Pallas kernels, local(): pl.pallas_call(body, out_shape=(jax.ShapeDtypeStruct((16, 1024), BF), jax...  109 us

profile of v2, /device:TPU:1, one launch (start us, length us, event | category | flops | bytes accessed | tf_op | source)
XLA Modules:
  0.0 111.9 jit_solution(2282239593394403364)
XLA Ops:
  0.6 109.1 %shard_map.95 = (bf16[16,1024]{1,0:T(8,128)(2,1)}, f32[1,16]{1,0:T(1,128)}) custom-call(bf16[16,16384]{1,0:T(8,128)(2,1)} %tokens.1, bf16[1024,1664]{1,0:T(8,128)(2,1)} %gc.1, bf16[8,3328]{1,0:T(8,128)(2,1)} %gs.1, bf16[1024,1664]{1,0:T(8,128)(2,1)} %uc.1, bf16[8,3328]{1,0:T(8,128)(2,1)} %us.1, bf16[3328,512]{1,0:T(8,128)(2,1)} %dc.1, bf16[26,1024]{1,0:T(8,128)(2,1)} %ds.1, ...), custom_call_target="tpu_custom_call" | custom-call | tf_op jit(solution)/shard_map/pallas_call | solution.py:484
  109.7 2.1 %shard_map.96 = (bf16[16,1024]{1,0:T(8,128)(2,1)}, f32[1,16]{1,0:T(1,128)}) custom-call(bf16[16,1024]{1,0:T(8,128)(2,1)} %get-tuple-element.6.a, f32[1,16]{1,0:T(1,128)} %get-tuple-element.7.b), custom_call_target="tpu_custom_call" | custom-call | tf_op jit(solution)/shard_map/pallas_call | solution.py:537

commit v3 on v2

--- a/solution.py
+++ b/solution.py
@@ -17,18 +17,11 @@
 F32 = jnp.float32
 
 NE = 9
-ZEND = 5
-NZF = (ZEND + 2) // 3
-LAG_Z = (2, 2)
-LAG_H = (6, 4)
-LAG_W = (7, 5)
-LAG_G = (8, 6)
-LAG_X = (10, 8)
-LAG_S = (12, 10)
-TICKS = max(NE + LAG_S[0], NB + LAG_S[1])
-T_SHARE = 2
-T_SIBLING = 8
-T_WORDS = min(LAG_S[0], NE + LAG_S[1])
+ZEND = 8
+NZF = ZEND // 2
+NG = 1
+ORDER = (131328, 318723, 2164229, 1050631, 657699, 1182501, 13644071, 3350540, 3478737, 3613394, 4265683, 4445232, 4528164, 4707634, 4215078, 14051806, 14103635, 4347176, 5757034, 7395638, 4512363, 7527224, 7986284, 7697265, 4618112, 9011834, 4751732, 8881539, 9075600, 7901814, 10058884, 9802641, 8817559, 8952480, 10654860, 9873819, 11591585, 10734744, 10990245, 11643577, 11252644, 12035765, 11844264, 11975867, 16777144)
+
 NOUT = 2
 
 
@@ -44,7 +37,7 @@
          x, gcv, ucv, dcv, own, xr, zr, zr2, xr2, hs, w1r, v, g, sw, st, dw, racc, rot, es, er, pk, pr,
          gsv, usv, dsv, sbp, sbt, wb, perm_in, perm_h, perm_out, walsh,
          code_sem, dcode_sem, loc_sem, a_send, a_recv, sib_sem, s1_send, s1_recv, s2_send, s2_recv,
-         s3_sem, x_send, x_recv, x2_send, x2_recv, z_send, z_recv, zz_send, zz_recv, w1_send, w1_recv, w2_send, w2_recv, g_send, g_recv,
+         s3_sem, x_send, x_recv, x2_send, x2_recv, z_send, z_recv, zz_send, zz_recv, gl_send, w1_send, w1_recv, w2_send, w2_recv, g_send, g_recv,
          gx_send, gx_recv, e_send, e_recv, p_send, p_recv):
     d = lax.axis_index("dp")
     t = lax.axis_index("tensor")
@@ -225,11 +218,11 @@
             st[16 * k:16 * k + 16, :] = jnp.where((words & (1 << k)) == 0, 1.0, -1.0).astype(BF)
 
     def z_first(c):
-        return (lax.rem(c, 3) == 0) & (c < ZEND)
+        return (lax.rem(c, 2) == 1) & (c < ZEND)
 
     def chain(c, step, first):
         sign = 1 - 2 * lax.rem(c, 2)
-        buf, ss, rs, m = (zr2, zz_send, zz_recv, c // 3) if first else (zr, z_send, z_recv, c)
+        buf, ss, rs, m = (zr2, zz_send, zz_recv, c // 2) if first else (zr, z_send, z_recv, c)
         for way, base, steps in ((1, 0, 4), (-1, 4, 3)):
             if step > steps:
                 continue
@@ -245,28 +238,30 @@
             remote(src, buf.at[m, base + step - 1], ss, rs.at[m, base + step - 1], to, t).start()
 
     def z_total(c, first):
-        buf, rs, m = (zr2, zz_recv, c // 3) if first else (zr, z_recv, c)
+        buf, rs, m = (zr2, zz_recv, c // 2) if first else (zr, z_recv, c)
         term = own[c, z] if first else own[c, z, xh]
         wait_bytes(buf.at[m, 3], rs.at[m, 3])
         wait_bytes(buf.at[m, 6], rs.at[m, 6])
         return term.astype(F32) + buf[m, 3].astype(F32) + buf[m, 6].astype(F32)
 
-    def z_step(step):
+    def chain_start(c):
+        add_partner(c)
+        chain(c, 1, False)
+
+    def chain_on(step):
         def stage(c):
             @pl.when(z_first(c))
             def _():
-                if step < 4:
-                    chain(c, step + 1, True)
-                else:
-                    own[c, z] = z_total(c, True).astype(BF)
-                    remote(own.at[c, z, 1 - xh], xr2.at[c // 3], x2_send, x2_recv.at[c // 3], partner, t).start()
+                chain(c, step, True)
 
             @pl.when(jnp.logical_not(z_first(c)))
             def _():
-                if step == 1:
-                    add_partner(c)
                 chain(c, step, False)
         return stage
+
+    def chain_end(c):
+        own[c, z] = z_total(c, True).astype(BF)
+        remote(own.at[c, z, 1 - xh], xr2.at[c // 2], x2_send, x2_recv.at[c // 2], partner, t).start()
 
     def add_partner(c):
         wait_bytes(xr.at[c], x_recv.at[c])
@@ -286,24 +281,24 @@
         gate, up = total[:, 0:256], total[:, 256:512]
         hs[c] = (gate / (1.0 + jnp.exp(-gate)) * up).astype(BF)
 
-    def hidden_chain(c):
+    def hidden(c):
         @pl.when(z_first(c))
         def _():
-            wait_bytes(xr2.at[c // 3], x2_recv.at[c // 3])
-            activate(c, own[c, z, xh].astype(F32) + xr2[c // 3].astype(F32))
-
-        @pl.when(jnp.logical_not(z_first(c)))
+            wait_bytes(xr2.at[c // 2], x2_recv.at[c // 2])
+            activate(c, own[c, z, xh].astype(F32) + xr2[c // 2].astype(F32))
+
+        @pl.when((c < NE) & jnp.logical_not(z_first(c)))
         def _():
             activate(c, z_total(c, False))
 
-        send_hidden(c)
-
-    def hidden_direct(c):
-        wait_bytes(zr.at[c], z_recv.at[c, 0])
-        total = own[c, z, xh].astype(F32)
-        for j in range(7):
-            total = total + zr[c, j].astype(F32)
-        activate(c, total)
+        @pl.when(c >= NE)
+        def _():
+            wait_bytes(zr.at[c], z_recv.at[c, 0])
+            total = own[c, z, xh].astype(F32)
+            for j in range(7):
+                total = total + zr[c, j].astype(F32)
+            activate(c, total)
+
         send_hidden(c)
 
     def send_hidden(c):
@@ -331,10 +326,23 @@
 
             lax.fori_loop(1, NT, send, 0)
 
+    def wait_mixed(b):
+        @pl.when(t != b)
+        def _():
+            wait_bytes(g.at[b, z, xh], w2_recv.at[b])
+
+    def gather_all(b):
+        wait_mixed(b)
+
+        def send(j, carry):
+            part = g.at[b, z, xh]
+            remote(part, part, gl_send, g_recv.at[b], lax.rem(d + j, NDP), t).start()
+            return carry
+
+        lax.fori_loop(1, NDP, send, 0)
+
     def gather_z(b):
-        @pl.when(t != b)
-        def _():
-            wait_bytes(g.at[b, z, xh], w2_recv.at[b])
+        wait_mixed(b)
 
         def send(j, carry):
             zz = lax.rem(z + j, 8)
@@ -349,58 +357,59 @@
         remote(half, half, gx_send, gx_recv.at[b], partner, t).start()
 
     def turn(b):
-        wait_bytes(g.at[b, :, 1 - xh], gx_recv.at[b])
+        @pl.when(b < NB - NG)
+        def _():
+            wait_bytes(g.at[b, :, 1 - xh], gx_recv.at[b])
+
+        @pl.when(b >= NB - NG)
+        def _():
+            wait_bytes(v.at[pl.ds(0, NDP - 1)], g_recv.at[b])
+
         unpack(b)
         left = g[b].reshape(256, 256)
         for n in range(NB):
             cols = slice(256 * n, 256 * n + 256)
             racc[:, cols] += jnp.dot(left, st[:, cols], preferred_element_type=F32)
 
-    def during(i, lag, stage, first, last):
-        @pl.when((i >= first + lag) & (i < last + lag))
-        def _():
-            stage(i - lag)
-
-    def each(i, lags, stage):
-        if lags[0] == lags[1]:
-            during(i, lags[0], stage, 0, NB)
-        else:
-            during(i, lags[0], stage, 0, NE)
-            during(i, lags[1], stage, NE, NB)
-
+    def aside(b):
+        @pl.when(b < NB)
+        def _():
+            down_weights(b)
+
+        @pl.when(b == 13)
+        def _():
+            share_words()
+
+        @pl.when(b == 14)
+        def _():
+            words_to_sibling()
+
+        @pl.when(b == 15)
+        def _():
+            words_of(1, s3_sem.at[1])
+
+    stages = (gate_up, chain_start, chain_on(2), chain_on(3), chain_on(4), chain_end, z_direct, hidden, mix, gather_z,
+              gather_x, turn, gather_all, aside)
     racc[...] = jnp.zeros_like(racc)
 
-    def tick(i, carry):
-        during(i, 0, gate_up, 0, NB)
-        if NE:
-            for step in range(1, 5):
-                during(i, LAG_Z[0] + step - 1, z_step(step), 0, NE)
-        during(i, LAG_Z[1], z_direct, NE, NB)
-        if NE:
-            during(i, LAG_H[0], hidden_chain, 0, NE)
-        during(i, LAG_H[1], hidden_direct, NE, NB)
-        each(i, LAG_W, mix)
-        each(i, LAG_G, gather_z)
-        each(i, LAG_X, gather_x)
-
-        @pl.when(i == T_SHARE)
-        def _():
-            share_words()
-
-        during(i, 1, down_weights, 0, NB)
-
-        @pl.when(i == T_SIBLING)
-        def _():
-            words_to_sibling()
-
-        @pl.when(i == T_WORDS)
-        def _():
-            words_of(1, s3_sem.at[1])
-
-        each(i, LAG_S, turn)
+    def three(i, carry):
+        codes = jnp.int32(0)
+        for k, number in enumerate(ORDER):
+            codes = jnp.where(i == k, number, codes)
+
+        def one(j, codes):
+            code = lax.rem(codes, 256)
+            block = lax.rem(code, 16)
+            for k, stage in enumerate(stages):
+                @pl.when(code // 16 == k)
+                def _():
+                    stage(block)
+            return codes // 256
+
+        lax.fori_loop(0, 3, one, codes)
         return carry
 
-    lax.fori_loop(0, TICKS, tick, 0)
+    lax.fori_loop(0, len(ORDER), three, 0)
 
     rot[...] = racc[...].astype(BF).reshape(16, 16, HB)
     top = jnp.max(jnp.abs(rot[d].astype(F32)), axis=1, keepdims=True)
@@ -455,6 +464,8 @@
     words_of(0, s3_sem.at[0])
     wait_bytes(xr.at[pl.ds(0, NB - NZF)], x_send)
     wait_bytes(zr.at[pl.ds(0, NB - NZF)], z_send)
+    if NG:
+        wait_bytes(v.at[pl.ds(0, NDP - 1)], gl_send)
     if NZF:
         wait_bytes(xr2, x2_send)
         wait_bytes(zr2, zz_send)
@@ -468,8 +479,8 @@
     def _():
         wait_bytes(hs, w1_send)
 
-    wait_bytes(g.at[:, pl.ds(0, 7), 0], g_send)
-    wait_bytes(g.at[:, :, 0], gx_send)
+    wait_bytes(g.at[pl.ds(0, NB - NG), pl.ds(0, 7), 0], g_send)
+    wait_bytes(g.at[pl.ds(0, NB - NG), :, 0], gx_send)
     for n in range(NOUT):
         wait_bytes(es.at[n, pl.ds(0, NT - 1)], e_send.at[n])
     wait_bytes(pr.at[pl.ds(0, NT - 1)], p_send)
@@ -520,7 +531,7 @@
             vm((256, 256), BF),
             vm((256, 256), BF),
             dma((2, NB)), dma, dma, dma, dma, dma((2,)), dma, dma, dma, dma((4,)),
-            dma((2,)), dma, dma((NB,)), dma, dma((max(NZF, 1),)), dma, dma((NB, 7)), dma, dma((max(NZF, 1), 7)), dma, dma, dma, dma((NB,)), dma, dma((NB,)),
+            dma((2,)), dma, dma((NB,)), dma, dma((max(NZF, 1),)), dma, dma((NB, 7)), dma, dma((max(NZF, 1), 7)), dma, dma, dma, dma, dma((NB,)), dma, dma((NB,)),
             dma, dma((NB,)), dma((NOUT,)), dma((NOUT,)), dma, dma,
         ],
         compiler_params=pltpu.CompilerParams(

time: 112 us -> 104 us (0.929)
  Pallas kernels: 111 us -> 103 us
    pallas_call x1, Pallas kernels: 109 us -> 101 us  [local(): pl.pallas_call(body, out_shape=(jax.ShapeDtypeStruct((16, 1024), BF), jax...]
where the time goes in v3:
time: 104 us
  Pallas kernels  103 us (99%)
    pallas_call x1, Pallas kernels, local(): pl.pallas_call(body, out_shape=(jax.ShapeDtypeStruct((16, 1024), BF), jax...  101 us
    pallas_call x1, Pallas kernels, local(): pl.pallas_call(hand_on, out_shape=(jax.ShapeDtypeStruct((16, 1024), BF),...  2.13 us

profile of v3, /device:TPU:1, one launch (start us, length us, event | category | flops | bytes accessed | tf_op | source)
XLA Modules:
  0.0 103.7 jit_solution(16959893723551122062)
XLA Ops:
  0.6 100.9 %shard_map.95 = (bf16[16,1024]{1,0:T(8,128)(2,1)}, f32[1,16]{1,0:T(1,128)}) custom-call(bf16[16,16384]{1,0:T(8,128)(2,1)} %tokens.1, bf16[1024,1664]{1,0:T(8,128)(2,1)} %gc.1, bf16[8,3328]{1,0:T(8,128)(2,1)} %gs.1, bf16[1024,1664]{1,0:T(8,128)(2,1)} %uc.1, bf16[8,3328]{1,0:T(8,128)(2,1)} %us.1, bf16[3328,512]{1,0:T(8,128)(2,1)} %dc.1, bf16[26,1024]{1,0:T(8,128)(2,1)} %ds.1, ...), custom_call_target="tpu_custom_call" | custom-call | tf_op jit(solution)/shard_map/pallas_call | solution.py:495
  101.6 2.1 %shard_map.96 = (bf16[16,1024]{1,0:T(8,128)(2,1)}, f32[1,16]{1,0:T(1,128)}) custom-call(bf16[16,1024]{1,0:T(8,128)(2,1)} %get-tuple-element.6.a, f32[1,16]{1,0:T(1,128)} %get-tuple-element.7.b), custom_call_target="tpu_custom_call" | custom-call | tf_op jit(solution)/shard_map/pallas_call | solution.py:548

commit v4 on v3

--- a/solution.py
+++ b/solution.py
@@ -1,3 +1,4 @@
+import functools
 import math
 
 import jax
@@ -16,13 +17,17 @@
 BF = jnp.bfloat16
 F32 = jnp.float32
 
-NE = 9
-ZEND = 8
-NZF = ZEND // 2
-NG = 1
-ORDER = (131328, 318723, 2164229, 1050631, 657699, 1182501, 13644071, 3350540, 3478737, 3613394, 4265683, 4445232, 4528164, 4707634, 4215078, 14051806, 14103635, 4347176, 5757034, 7395638, 4512363, 7527224, 7986284, 7697265, 4618112, 9011834, 4751732, 8881539, 9075600, 7901814, 10058884, 9802641, 8817559, 8952480, 10654860, 9873819, 11591585, 10734744, 10990245, 11643577, 11252644, 12035765, 11844264, 11975867, 16777144)
+ZFIRST = (0, 1, 3, 4, 6, 8, 11)
+DIRECT = ()
+WIDE = (10, 12)
+NZF = len(ZFIRST)
+ORDER = (131328, 318723, 401413, 2295585, 599048, 1232944, 3221002, 3345361, 2627026, 13841420, 1516096, 4314166, 2442027, 13973529, 3297348, 1714134, 3887430, 5496535, 2742325, 7358492, 3621460, 5647065, 4541297, 14301555, 7493676, 7620480, 7789370, 5993857, 3965769, 7895004, 8669826, 8812944, 5012357, 8033169, 9603207, 9010324, 9803403, 9931424, 9214113, 10197411, 11591586, 11651748, 11783334, 10990245, 11118772, 11905974, 12236983, 12368825)
 
 NOUT = 2
+
+
+def among(c, blocks):
+    return functools.reduce(jnp.logical_or, [c == k for k in blocks], c < 0)
 
 
 def eo_column(p):
@@ -121,6 +126,8 @@
     odd = (both ^ (both >> 1) ^ (both >> 2) ^ (both >> 3)) & 1
     walsh[...] = jnp.where((src & 15) == (dst & 15), jnp.where(odd == 1, -1.0, 1.0), 0.0).astype(BF)
 
+    racc[...] = jnp.zeros_like(racc)
+
     for b in range(NB):
         cols = slice(256 * b, 256 * b + 256)
         gsv[b] = jnp.dot(gs[:, cols], perm_in[...], preferred_element_type=F32)
@@ -218,11 +225,11 @@
             st[16 * k:16 * k + 16, :] = jnp.where((words & (1 << k)) == 0, 1.0, -1.0).astype(BF)
 
     def z_first(c):
-        return (lax.rem(c, 2) == 1) & (c < ZEND)
+        return among(c, ZFIRST)
 
     def chain(c, step, first):
         sign = 1 - 2 * lax.rem(c, 2)
-        buf, ss, rs, m = (zr2, zz_send, zz_recv, c // 2) if first else (zr, z_send, z_recv, c)
+        buf, ss, rs, m = (zr2, zz_send, zz_recv, c) if first else (zr, z_send, z_recv, c)
         for way, base, steps in ((1, 0, 4), (-1, 4, 3)):
             if step > steps:
                 continue
@@ -238,7 +245,7 @@
             remote(src, buf.at[m, base + step - 1], ss, rs.at[m, base + step - 1], to, t).start()
 
     def z_total(c, first):
-        buf, rs, m = (zr2, zz_recv, c // 2) if first else (zr, z_recv, c)
+        buf, rs, m = (zr2, zz_recv, c) if first else (zr, z_recv, c)
         term = own[c, z] if first else own[c, z, xh]
         wait_bytes(buf.at[m, 3], rs.at[m, 3])
         wait_bytes(buf.at[m, 6], rs.at[m, 6])
@@ -261,7 +268,7 @@
 
     def chain_end(c):
         own[c, z] = z_total(c, True).astype(BF)
-        remote(own.at[c, z, 1 - xh], xr2.at[c // 2], x2_send, x2_recv.at[c // 2], partner, t).start()
+        remote(own.at[c, z, 1 - xh], xr2.at[c], x2_send, x2_recv.at[c], partner, t).start()
 
     def add_partner(c):
         wait_bytes(xr.at[c], x_recv.at[c])
@@ -284,14 +291,14 @@
     def hidden(c):
         @pl.when(z_first(c))
         def _():
-            wait_bytes(xr2.at[c // 2], x2_recv.at[c // 2])
-            activate(c, own[c, z, xh].astype(F32) + xr2[c // 2].astype(F32))
-
-        @pl.when((c < NE) & jnp.logical_not(z_first(c)))
+            wait_bytes(xr2.at[c], x2_recv.at[c])
+            activate(c, own[c, z, xh].astype(F32) + xr2[c].astype(F32))
+
+        @pl.when(jnp.logical_not(among(c, ZFIRST + DIRECT)))
         def _():
             activate(c, z_total(c, False))
 
-        @pl.when(c >= NE)
+        @pl.when(among(c, DIRECT))
         def _():
             wait_bytes(zr.at[c], z_recv.at[c, 0])
             total = own[c, z, xh].astype(F32)
@@ -336,7 +343,7 @@
 
         def send(j, carry):
             part = g.at[b, z, xh]
-            remote(part, part, gl_send, g_recv.at[b], lax.rem(d + j, NDP), t).start()
+            remote(part, part, gl_send.at[b], g_recv.at[b], lax.rem(d + j, NDP), t).start()
             return carry
 
         lax.fori_loop(1, NDP, send, 0)
@@ -357,11 +364,11 @@
         remote(half, half, gx_send, gx_recv.at[b], partner, t).start()
 
     def turn(b):
-        @pl.when(b < NB - NG)
+        @pl.when(jnp.logical_not(among(b, WIDE)))
         def _():
             wait_bytes(g.at[b, :, 1 - xh], gx_recv.at[b])
 
-        @pl.when(b >= NB - NG)
+        @pl.when(among(b, WIDE))
         def _():
             wait_bytes(v.at[pl.ds(0, NDP - 1)], g_recv.at[b])
 
@@ -390,8 +397,6 @@
 
     stages = (gate_up, chain_start, chain_on(2), chain_on(3), chain_on(4), chain_end, z_direct, hidden, mix, gather_z,
               gather_x, turn, gather_all, aside)
-    racc[...] = jnp.zeros_like(racc)
-
     def three(i, carry):
         codes = jnp.int32(0)
         for k, number in enumerate(ORDER):
@@ -464,11 +469,11 @@
     words_of(0, s3_sem.at[0])
     wait_bytes(xr.at[pl.ds(0, NB - NZF)], x_send)
     wait_bytes(zr.at[pl.ds(0, NB - NZF)], z_send)
-    if NG:
-        wait_bytes(v.at[pl.ds(0, NDP - 1)], gl_send)
+    for b in WIDE:
+        wait_bytes(v.at[pl.ds(0, NDP - 1)], gl_send.at[b])
     if NZF:
-        wait_bytes(xr2, x2_send)
-        wait_bytes(zr2, zz_send)
+        wait_bytes(xr2.at[pl.ds(0, NZF)], x2_send)
+        wait_bytes(zr2.at[pl.ds(0, NZF)], zz_send)
 
     @pl.when(t < NB)
     def _():
@@ -479,8 +484,8 @@
     def _():
         wait_bytes(hs, w1_send)
 
-    wait_bytes(g.at[pl.ds(0, NB - NG), pl.ds(0, 7), 0], g_send)
-    wait_bytes(g.at[pl.ds(0, NB - NG), :, 0], gx_send)
+    wait_bytes(g.at[pl.ds(0, NB - len(WIDE)), pl.ds(0, 7), 0], g_send)
+    wait_bytes(g.at[pl.ds(0, NB - len(WIDE)), :, 0], gx_send)
     for n in range(NOUT):
         wait_bytes(es.at[n, pl.ds(0, NT - 1)], e_send.at[n])
     wait_bytes(pr.at[pl.ds(0, NT - 1)], p_send)
@@ -505,8 +510,8 @@
             vm((NB, 8, 2, 16, 512), BF),
             vm((NB, 8, 16, 512), BF),
             vm((NB, 7, 16, 512), BF),
-            vm((max(NZF, 1), 7, 2, 16, 512), BF),
-            vm((max(NZF, 1), 16, 512), BF),
+            vm((NB, 7, 2, 16, 512), BF),
+            vm((NB, 16, 512), BF),
             vm((NB, 16, 256), BF),
             vm((16, 16, 256), BF),
             vm((16, 16, 256), BF),
@@ -531,7 +536,7 @@
             vm((256, 256), BF),
             vm((256, 256), BF),
             dma((2, NB)), dma, dma, dma, dma, dma((2,)), dma, dma, dma, dma((4,)),
-            dma((2,)), dma, dma((NB,)), dma, dma((max(NZF, 1),)), dma, dma((NB, 7)), dma, dma((max(NZF, 1), 7)), dma, dma, dma, dma, dma((NB,)), dma, dma((NB,)),
+            dma((2,)), dma, dma((NB,)), dma, dma((NB,)), dma, dma((NB, 7)), dma, dma((NB, 7)), dma((NB,)), dma, dma, dma, dma((NB,)), dma, dma((NB,)),
             dma, dma((NB,)), dma((NOUT,)), dma((NOUT,)), dma, dma,
         ],
         compiler_params=pltpu.CompilerParams(

time: 104 us -> 101 us (0.971)
  Pallas kernels: 103 us -> 100 us
    pallas_call x1, Pallas kernels: 101 us -> 97.9 us  [local(): pl.pallas_call(body, out_shape=(jax.ShapeDtypeStruct((16, 1024), BF), jax...]
where the time goes in v4:
time: 101 us
  Pallas kernels  100 us (99%)
    pallas_call x1, Pallas kernels, local(): pl.pallas_call(body, out_shape=(jax.ShapeDtypeStruct((16, 1024), BF), jax...  97.9 us
    pallas_call x1, Pallas kernels, local(): pl.pallas_call(hand_on, out_shape=(jax.ShapeDtypeStruct((16, 1024), BF),...  2.13 us

profile of v4, /device:TPU:1, one launch (start us, length us, event | category | flops | bytes accessed | tf_op | source)
XLA Modules:
  0.0 100.7 jit_solution(4637800433379095582)
XLA Ops:
  0.6 97.9 %shard_map.95 = (bf16[16,1024]{1,0:T(8,128)(2,1)}, f32[1,16]{1,0:T(1,128)}) custom-call(bf16[16,16384]{1,0:T(8,128)(2,1)} %tokens.1, bf16[1024,1664]{1,0:T(8,128)(2,1)} %gc.1, bf16[8,3328]{1,0:T(8,128)(2,1)} %gs.1, bf16[1024,1664]{1,0:T(8,128)(2,1)} %uc.1, bf16[8,3328]{1,0:T(8,128)(2,1)} %us.1, bf16[3328,512]{1,0:T(8,128)(2,1)} %dc.1, bf16[26,1024]{1,0:T(8,128)(2,1)} %ds.1, ...), custom_call_target="tpu_custom_call" | custom-call | tf_op jit(solution)/shard_map/pallas_call | solution.py:500
  98.5 2.1 %shard_map.96 = (bf16[16,1024]{1,0:T(8,128)(2,1)}, f32[1,16]{1,0:T(1,128)}) custom-call(bf16[16,1024]{1,0:T(8,128)(2,1)} %get-tuple-element.6.a, f32[1,16]{1,0:T(1,128)} %get-tuple-element.7.b), custom_call_target="tpu_custom_call" | custom-call | tf_op jit(solution)/shard_map/pallas_call | solution.py:553

commit v5 on v4

--- a/solution.py
+++ b/solution.py
@@ -19,9 +19,9 @@
 
 ZFIRST = (0, 1, 3, 4, 6, 8, 11)
 DIRECT = ()
-WIDE = (10, 12)
+WIDE = (12,)
 NZF = len(ZFIRST)
-ORDER = (131328, 318723, 401413, 2295585, 599048, 1232944, 3221002, 3345361, 2627026, 13841420, 1516096, 4314166, 2442027, 13973529, 3297348, 1714134, 3887430, 5496535, 2742325, 7358492, 3621460, 5647065, 4541297, 14301555, 7493676, 7620480, 7789370, 5993857, 3965769, 7895004, 8669826, 8812944, 5012357, 8033169, 9603207, 9010324, 9803403, 9931424, 9214113, 10197411, 11591586, 11651748, 11783334, 10990245, 11118772, 11905974, 12236983, 12368825)
+ORDER = (131328, 318723, 401413, 2295585, 599048, 1232944, 3221002, 3345361, 2627026, 13841420, 1516096, 4314166, 2442027, 13973529, 3297348, 1714134, 3887430, 5496535, 2742325, 7358492, 3621460, 5647065, 4541297, 14301555, 7493676, 7620480, 7789370, 5993857, 3965769, 7895004, 8669826, 8812944, 5012357, 8033169, 9603207, 9010324, 9803403, 9931424, 9214113, 10197411, 11591586, 11639460, 11783334, 10990245, 11118772, 11905974, 12105642, 12303545, 16777146)
 
 NOUT = 2
 
@@ -100,7 +100,7 @@
         return tokens.at[:, lanes]
 
     def send_tokens(j, carry):
-        to = lax.rem(d + j, NDP)
+        to = lax.rem(d + 1 + lax.rem(j + 5, NDP - 1), NDP)
         remote(token_copy(to), x.at[core, d], a_send, a_recv, to, t).start()
         return carry
 

time: 101 us -> 101 us (level)
  no operation moved by 1% of the time
where the time goes in v5:
time: 101 us
  Pallas kernels  99.9 us (99%)
    pallas_call x1, Pallas kernels, local(): pl.pallas_call(body, out_shape=(jax.ShapeDtypeStruct((16, 1024), BF), jax...  97.8 us
    pallas_call x1, Pallas kernels, local(): pl.pallas_call(hand_on, out_shape=(jax.ShapeDtypeStruct((16, 1024), BF),...  2.13 us

profile of v5, /device:TPU:1, one launch (start us, length us, event | category | flops | bytes accessed | tf_op | source)
XLA Modules:
  0.0 100.5 jit_solution(5165797354263986909)
XLA Ops:
  0.6 97.8 %shard_map.95 = (bf16[16,1024]{1,0:T(8,128)(2,1)}, f32[1,16]{1,0:T(1,128)}) custom-call(bf16[16,16384]{1,0:T(8,128)(2,1)} %tokens.1, bf16[1024,1664]{1,0:T(8,128)(2,1)} %gc.1, bf16[8,3328]{1,0:T(8,128)(2,1)} %gs.1, bf16[1024,1664]{1,0:T(8,128)(2,1)} %uc.1, bf16[8,3328]{1,0:T(8,128)(2,1)} %us.1, bf16[3328,512]{1,0:T(8,128)(2,1)} %dc.1, bf16[26,1024]{1,0:T(8,128)(2,1)} %ds.1, ...), custom_call_target="tpu_custom_call" | custom-call | tf_op jit(solution)/shard_map/pallas_call | solution.py:500
  98.4 2.1 %shard_map.96 = (bf16[16,1024]{1,0:T(8,128)(2,1)}, f32[1,16]{1,0:T(1,128)}) custom-call(bf16[16,1024]{1,0:T(8,128)(2,1)} %get-tuple-element.6.a, f32[1,16]{1,0:T(1,128)} %get-tuple-element.7.b), custom_call_target="tpu_custom_call" | custom-call | tf_op jit(solution)/shard_map/pallas_call | solution.py:553
